TPU v7x, 32 devices: a whole 2x2x4 slice. The times are simulated.
32 devices in a mesh: fsdp: 8 (over y, x, core), tensor: 4 (over z).
Axes of the slice: x: 2, y: 2, z: 4, core: 2. Of those that a mesh axis runs over, the one named last changes fastest.
Arguments:
- tokens: bfloat16 [1024, 8192], P('tensor', 'fsdp'), may hold values from -6 to 6
- gate_weight: bfloat16 [8192, 14336], P('fsdp', 'tensor'), may hold values from -0.0625 to 0.0625
- up_weight: bfloat16 [8192, 14336], P('fsdp', 'tensor'), may hold values from -0.0625 to 0.0625
- down_frozen: bfloat16 [14336, 8192], P('tensor', 'fsdp'), may hold values from -0.046875 to 0.046875
- down_learn: bfloat16 [14336, 8192], P('tensor', 'fsdp'), may hold values from -0.046875 to 0.046875
- steer: float32 [8192], replicated, may hold values from -6 to 6
- sample_lengths: int32 [2, 4], replicated, may hold values from 1 to 128, 320 in all within a row
Outputs:
- grad_down: float32 [14336, 8192], P('tensor', 'fsdp')
- losses: float32 [2], replicated
Inputs may be any that keep to these rules, and one draw needn't show every extreme that they name: `sample_lengths`: in each row, the lengths sum to 320 and one sample has exactly 128 live tokens.
All inputs are finite; a program needn't handle non-finite values.
Results may differ from a plain program's by a relative error of at most 0.0047.
Values may be sent and summed in bfloat16 or wider, within the bound.
No kernel may reach another device: no remote copies, remote signals or barrier semaphores. Data moves between devices by JAX's collectives and lax.ppermute only.
A program may use at most 128 MiB of HBM per device.

v0:
```python
import math

import jax
import jax.numpy as jnp
from jax import lax
from jax.experimental import pallas as pl
from jax.experimental.pallas import tpu as pltpu
from jax.sharding import PartitionSpec as P

D = 8192
SLOT = 128
TOKEN_BOUND = 6.0
WEIGHT_BOUND = 0.0625
HALF_MAX = 65504.0
SIB_PARTS = 2
GRAD_VMEM_BYTES = 56 * 1024 * 1024
IN_VMEM_BYTES = 40 * 1024 * 1024
f32 = jnp.float32
bf16 = jnp.bfloat16
f16 = jnp.float16
FREE = pl.CostEstimate(flops=0, bytes_accessed=0, transcendentals=0)
FIRST = (2, 4)
SECOND = (4, 2)


def slot_lengths(slot_ids, flat, sample_count):
    sample_ids = jnp.arange(sample_count, dtype=jnp.int32)
    return jnp.sum(jnp.where(slot_ids[:, None] == sample_ids[None, :], flat[None, :], 0), axis=1)


def dot(a, b):
    return jnp.dot(a, b, preferred_element_type=f32)


def swap(axis, bit, x):
    return lax.ppermute(x, axis, [(i, i ^ bit) for i in range(lax.axis_size(axis))])


def by_core(axis_bits, x):
    even, odd = axis_bits
    n = lax.axis_size("fsdp")
    return lax.ppermute(x, "fsdp", [(i, i ^ (odd if i % 2 else even)) for i in range(n)])


def after(x, *others):
    return lax.optimization_barrier((x,) + others)[0]


def in_kernel(core_ref, x1_ref, x2_ref, s1_ref, s2_ref, wg_ref, wu_ref, *refs, scale):
    x = jnp.concatenate([x1_ref[...], x2_ref[...]], axis=0)
    xs = jnp.concatenate([s1_ref[...], s2_ref[...]], axis=0)
    *sibs, out_ref = refs
    n = len(sibs) // 2
    depth = x.shape[1] // n
    for i, own_ref in enumerate((wg_ref, wu_ref)):
        total = dot(x, own_ref[...])
        for k, sib_ref in enumerate(sibs[i * n : (i + 1) * n]):
            total += dot(xs[:, k * depth : (k + 1) * depth], sib_ref[...])
        out_ref[i] = total * scale


def in_products(core, first, first_at, second, second_at, weights, quarter, scale, cost):
    gate_weight, up_weight, gate_sib, up_sib = weights
    cols = first[0].shape[1]
    depth, half = gate_sib[0].shape
    steps = 2
    tile = half // steps
    rows1 = pl.BlockSpec((quarter, cols), lambda j, c: (first_at(c[0]), 0))
    rows2 = pl.BlockSpec((quarter, cols), lambda j, c: (second_at(c[0]), 0))
    own = pl.BlockSpec((cols, tile), lambda j, c: (0, c[0] * steps + j))
    sib = pl.BlockSpec((depth, tile), lambda j, c: (0, j))
    return pl.pallas_call(
        lambda *refs: in_kernel(*refs, scale=scale),
        grid_spec=pltpu.PrefetchScalarGridSpec(
            num_scalar_prefetch=1,
            grid=(steps,),
            in_specs=[rows1, rows2, rows1, rows2, own, own] + [sib] * (2 * len(gate_sib)),
            out_specs=pl.BlockSpec((2, 2 * quarter, tile), lambda j, c: (0, 0, j)),
        ),
        out_shape=jax.ShapeDtypeStruct((2, 2 * quarter, half), f32),
        compiler_params=pltpu.CompilerParams(vmem_limit_bytes=IN_VMEM_BYTES),
        cost_estimate=cost,
        name="in_products",
    )(core, first[0], second[0], first[1], second[1], gate_weight, up_weight, *gate_sib, *up_sib)


def grad_kernel(*refs):
    *operands, out_ref = refs
    n = len(operands) // 2
    hidden = jnp.concatenate([h[...] for h in operands[:n]], axis=0)
    delta = jnp.concatenate([d[...] for d in operands[n:]], axis=0)
    out_ref[...] = lax.dot_general(
        hidden, delta, (((0,), (0,)), ((), ())), preferred_element_type=f32
    )


def grad_products(hiddens, deltas):
    width, cols = hiddens[0].shape[1], deltas[0].shape[1]
    steps = 4
    tile = width // steps
    specs = [pl.BlockSpec((h.shape[0], tile), lambda j: (0, j)) for h in hiddens]
    specs += [pl.BlockSpec(d.shape, lambda j: (0, 0)) for d in deltas]
    return pl.pallas_call(
        grad_kernel,
        grid=(steps,),
        in_specs=specs,
        out_specs=pl.BlockSpec((tile, cols), lambda j: (j, 0)),
        out_shape=jax.ShapeDtypeStruct((width, cols), f32),
        compiler_params=pltpu.CompilerParams(vmem_limit_bytes=GRAD_VMEM_BYTES),
        cost_estimate=FREE,
        name="grad_products",
    )(*hiddens, *deltas)


def paired_shards(tokens, gate_weight, up_weight, down_frozen, down_learn, steer, sample_lengths):
    cols = tokens.shape[1]
    slots = tokens.shape[0]
    half = gate_weight.shape[1] // 2
    seqs = sample_lengths.shape[1]
    rows = seqs * SLOT * 5 // 8
    own_rows, quarter = rows // 2, rows // 4
    total = cols * lax.axis_size("fsdp")
    scale = 2.0 ** math.floor(math.log2(HALF_MAX / (TOKEN_BOUND * WEIGHT_BOUND * total)))
    me_f = lax.axis_index("fsdp")
    me_t = lax.axis_index("tensor")
    core = me_f % 2
    chip = me_f // 2
    forget_first = me_t // 2 == 0
    low_half = (me_t % 2) == (me_t // 2)
    even = core == 0
    core_arg = core.reshape(1).astype(jnp.int32)

    other_tokens = swap("tensor", 1, tokens)

    def traded(w, sent):
        depth = cols // SIB_PARTS
        parts = []
        for k in range(SIB_PARTS):
            at = (k * depth, (1 - core) * half)
            sent.append(lax.dynamic_slice(after(w, *sent[-1:]), at, (depth, half)))
            parts.append(swap("fsdp", 1, sent[-1]))
        return parts

    sent = []
    gate_sib = traded(gate_weight, sent)
    up_sib = traded(up_weight, sent)
    weights = (gate_weight, up_weight, gate_sib, up_sib)

    lengths = jnp.where(forget_first, sample_lengths[0], sample_lengths[1])
    before = jnp.cumsum(lengths) - lengths

    def pick(block_of_slots):
        slot_ids = block_of_slots * slots + jnp.arange(slots, dtype=jnp.int32)
        sample = slot_ids // SLOT
        inside = slot_ids % SLOT
        position = slot_lengths(sample, before, seqs) + inside
        position = jnp.where(inside < slot_lengths(sample, lengths, seqs), position, -1)
        row = jnp.arange(rows, dtype=jnp.int32)
        wanted = jnp.bitwise_xor(chip, row // quarter) * quarter + row % quarter
        return (wanted[:, None] == position[None, :]).astype(bf16)

    mine = me_t % 2
    mine_rows = dot(pick(mine), after(tokens, sent[-1]))
    other_tokens = after(other_tokens, mine_rows)
    x_a = (mine_rows + dot(pick(1 - mine), other_tokens)).astype(bf16)
    hi_b = swap("tensor", 3, x_a[quarter:])
    lo_b = swap("tensor", 3, x_a[:quarter])
    frozen_a = jnp.where(forget_first, 0.0, 1.0)
    frozen_b = 1.0 - frozen_a
    latest = []

    def go(*xs):
        out = lax.optimization_barrier(xs + tuple(latest))[: len(xs)]
        return out[0] if len(xs) == 1 else out

    def did(x):
        latest[:] = [x]
        return x

    class Chunk:
        def __init__(self, lo, hi, at):
            self.lo, self.hi, self.at = lo, hi, at

        def exchange(self):
            self.hi = did(go(self.hi))
            self.hi_sib = swap("fsdp", 1, self.hi)
            if self.lo is None:
                self.lo, self.lo_sib = self.hi, self.hi_sib

        def exchange_lo(self):
            self.lo = did(go(self.lo))
            self.lo_sib = swap("fsdp", 1, self.lo)

        def products(self, cost):
            hi, at = go(self.hi, self.hi_sib), self.at
            self.give = did(
                in_products(
                    core_arg, hi, lambda c: at + c, hi, lambda c: at + 2, weights, quarter, scale, cost
                )
            )

        def send(self, apart):
            give = go(self.give)
            if apart:
                gives = [give[k, r : r + quarter].astype(f16) for k in range(2) for r in (0, quarter)]
                did(gives[-1])
                self.got = [by_core(FIRST, g) for g in gives]
            else:
                got = by_core(FIRST, did(give.astype(f16)))
                self.got = [got[k, r : r + quarter] for k in range(2) for r in (0, quarter)]

        def keep(self, cost):
            lo, lo_sib, hi, hi_sib = go(self.lo, self.lo_sib, self.hi, self.hi_sib)
            at = self.at
            self.kept = did(
                in_products(
                    core_arg, (lo, lo_sib), lambda c: 0, (hi, hi_sib), lambda c: at + 1 - c, weights, quarter, scale, cost
                )
            )

        def second(self):
            *got, kept = go(*self.got, self.kept)
            gives = [kept[k, quarter:] + got[2 * k + 1].astype(f32) for k in range(2)]
            give = did(jnp.concatenate(gives, axis=0).astype(f16))
            self.kept = [kept[k, :quarter] + got[2 * k].astype(f32) for k in range(2)]
            self.got = by_core(SECOND, give)

        def hidden(self):
            got, gate, up = go(self.got, *self.kept)
            gate = (gate + got[:quarter].astype(f32)) * (1.0 / scale)
            up = (up + got[quarter:].astype(f32)) * (1.0 / scale)
            self.own = did((jax.nn.silu(gate) * up).astype(bf16))
            self.got = by_core(SECOND, self.own)

        def gather_half(self):
            own, got = go(self.own, self.got)
            self.own = did(jnp.concatenate([own, got], axis=0))
            self.got = by_core(FIRST, self.own)
            self.own_sib = swap("fsdp", 1, self.own)

        def gather_whole(self):
            self.got = did(go(self.got))
            self.got_sib = swap("fsdp", 1, self.got)

        def down(self, frozen_part):
            own, got, own_sib, got_sib = go(self.own, self.got, self.own_sib, self.got_sib)

            def rows_of(want):
                def pick_rows(o, g, is_even):
                    low = jnp.concatenate([o[:quarter], jnp.where(is_even, g[:quarter], o[quarter:])], axis=0)
                    high = jnp.concatenate([jnp.where(is_even, o[quarter:], g[:quarter]), g[quarter:]], axis=0)
                    return jnp.where(want, low, high)

                mine = pick_rows(own, got, even)
                theirs = pick_rows(own_sib, got_sib, jnp.logical_not(even))
                return jnp.concatenate(
                    [jnp.where(even, mine, theirs), jnp.where(even, theirs, mine)], axis=1
                )

            def mlp(rows_in):
                return dot(rows_in, down_learn) - frozen_part * dot(rows_in, down_frozen)

            other_rows = rows_of(jnp.logical_not(low_half))
            own_rows_in = rows_of(low_half)
            give = did(mlp(other_rows).astype(bf16))
            self.got = swap("tensor", 1, give)
            self.parts = [own_rows_in, other_rows]
            self.rest = mlp

        def down_rest(self):
            self.mlp = did(self.rest(go(self.parts[0])))


        def pair(self):
            mlp, got = go(self.mlp, self.got)
            give = did((mlp + got.astype(f32)).astype(bf16))
            self.far = swap("tensor", 3, give)

        def delta(self, far):
            mlp, got, far = go(self.mlp, self.got, far)
            mlp = mlp + got.astype(f32) + far.astype(f32)
            x = jnp.concatenate([self.lo, self.hi], axis=0)
            base = jnp.where(low_half, x[:own_rows], x[own_rows:]).astype(f32)
            diff = jnp.where(forget_first, mlp, base + mlp - target[None, :])
            self.loss = jnp.sum(diff * diff)
            mine = did((diff * jnp.where(forget_first, 2.0, 1.0)).astype(bf16))
            self.back = swap("tensor", 3, mine)
            self.delta_b = [mine, swap("tensor", 1, mine)]

        def turn_back(self):
            back = did(go(self.back))
            self.delta_a = [back, swap("tensor", 1, back)]
            self.delta_b[1] = did(go(self.delta_b[1]))

    mean_square = jnp.mean(steer * steer)
    target_scale = 20.0 / jnp.sqrt(total * (mean_square + 1e-06))
    target = target_scale * lax.dynamic_slice_in_dim(steer, me_f * cols, cols)

    a, b = Chunk(None, x_a, 1), Chunk(lo_b, hi_b, 0)
    a.exchange()
    a.products(FREE)
    a.send(True)
    a.keep(FREE)
    b.exchange()
    a.second()
    b.products(FREE)
    a.hidden()
    b.send(False)
    b.exchange_lo()
    a.gather_half()
    b.keep(FREE)
    a.gather_whole()
    b.second()
    a.down(frozen_a)
    b.hidden()
    a.down_rest()
    b.gather_half()
    a.pair()
    b.gather_whole()
    b.down(frozen_b)
    b.down_rest()
    b.delta(a.far)
    value = jnp.full((8, 128), b.loss, f32)
    value = did(value + go(swap("fsdp", 2, value)))
    hiddens = go(*a.parts, *b.parts)
    did(hiddens[0])
    b.turn_back()
    for bit in (4, 1):
        value = did(value + go(swap("fsdp", bit, value)))
    b.delta_a[1] = did(go(b.delta_a[1]))
    others = [swap("tensor", bit, value) for bit in (1, 2, 3)]
    grad_down = did(grad_products(hiddens, go(*b.delta_a, *b.delta_b)))
    value, *others = go(value, *others)
    same, other = (value + others[0])[0, :2], (others[1] + others[2])[0, :2]
    steer_place = jnp.arange(2, dtype=jnp.int32) == 0
    counts = jnp.sum(sample_lengths, axis=1).astype(f32) * total
    losses = jnp.where(steer_place == forget_first, other, same) / counts
    return grad_down, losses


def gathered_shards(tokens, gate_weight, up_weight, down_frozen, down_learn, steer, sample_lengths):
    rows_tp = tokens.shape[0]
    cols = tokens.shape[1]
    width_ff = gate_weight.shape[1]
    n_tensor = lax.axis_size("tensor")
    total_rows = rows_tp * n_tensor
    seq_count = sample_lengths.shape[1]
    flat = sample_lengths.reshape(-1)
    gathered = lax.all_gather(tokens, "tensor", axis=0, tiled=True)
    every_slot = jnp.arange(total_rows, dtype=jnp.int32)
    every_len = slot_lengths(every_slot // SLOT, flat, 2 * seq_count)
    dead_key = jnp.where(every_slot % SLOT < every_len, 0, 1).astype(jnp.int32)
    live_total = 2 * (seq_count * SLOT * 5 // 8)
    source_ids = jnp.argsort(dead_key, stable=True)[:live_total]
    work_rows = jnp.take(gathered, source_ids, axis=0)
    count_rows = work_rows.shape[0]
    both_in = jnp.concatenate([gate_weight, up_weight], axis=1)
    block = work_rows
    summed = lax.psum_scatter(
        jnp.dot(block, both_in, preferred_element_type=jnp.float32),
        "fsdp",
        scatter_dimension=0,
        tiled=True,
    )
    hidden_own = (jax.nn.silu(summed[:, :width_ff]) * summed[:, width_ff:]).astype(jnp.bfloat16)
    hidden_all = lax.all_gather(hidden_own, "fsdp", axis=0, tiled=True)
    both_out = jnp.concatenate([down_frozen, down_learn], axis=1)
    own_count = count_rows // n_tensor
    block = hidden_all
    mlp_terms = lax.psum_scatter(
        jnp.dot(block, both_out, preferred_element_type=jnp.float32),
        "tensor",
        scatter_dimension=0,
        tiled=True,
    )
    own_start = lax.axis_index("tensor") * own_count
    base = lax.dynamic_slice_in_dim(work_rows, own_start, own_count, 0).astype(jnp.float32)
    out_frozen = base + mlp_terms[:, :cols]
    out_learn = base + mlp_terms[:, cols:]
    row_ids = lax.dynamic_slice_in_dim(source_ids, own_start, own_count, 0)
    row_len = slot_lengths(row_ids // SLOT, flat, 2 * seq_count)
    live = row_ids % SLOT < row_len
    forget = (live & (row_ids < seq_count * SLOT))[:, None]
    retain = (live & (row_ids >= seq_count * SLOT))[:, None]
    scale = 20.0 / jnp.sqrt(D * (jnp.mean(steer * steer) + 1e-06))
    target = scale * lax.dynamic_slice_in_dim(steer, lax.axis_index("fsdp") * cols, cols)
    steer_diff = out_learn - target[None, :]
    keep_diff = out_learn - out_frozen
    zero = jnp.zeros((), jnp.float32)
    local_steer = jnp.sum(jnp.where(forget, steer_diff * steer_diff, zero))
    local_keep = jnp.sum(jnp.where(retain, keep_diff * keep_diff, zero))
    sum_steer, sum_keep = lax.psum((local_steer, local_keep), ("fsdp", "tensor"))
    count_f = jnp.sum(sample_lengths[0]).astype(jnp.float32)
    count_r = jnp.sum(sample_lengths[1]).astype(jnp.float32)
    losses = jnp.stack([sum_steer / (count_f * D), sum_keep / (count_r * D)])
    delta = (jnp.where(forget, steer_diff, zero) + 2.0 * jnp.where(retain, keep_diff, zero)).astype(
        jnp.bfloat16
    )
    delta_all = lax.all_gather(delta, "tensor", axis=0, tiled=True)
    grad_down = lax.dot_general(
        hidden_all, delta_all, (((0,), (0,)), ((), ())), preferred_element_type=jnp.float32
    )
    return (grad_down, losses)


def solution(mesh):
    paired = mesh.shape["fsdp"] == 8 and mesh.shape["tensor"] == 4
    return jax.shard_map(
        paired_shards if paired else gathered_shards,
        mesh=mesh,
        in_specs=(
            P("tensor", "fsdp"),
            P("fsdp", "tensor"),
            P("fsdp", "tensor"),
            P("tensor", "fsdp"),
            P("tensor", "fsdp"),
            P(),
            P(),
        ),
        out_specs=(P("tensor", "fsdp"), P()),
        check_vma=False,
    )
```

profile of v0, /device:TPU:0, one launch (start us, length us, event | category | flops | bytes accessed | tf_op | source)
XLA Modules:
  0.0 170.1 jit_solution(18011515617499351154)
XLA Ops:
  0.6 3.1 %collective-permute-start = (bf16[256,1024]{1,0:T(8,128)(2,1)}, bf16[256,1024]{1,0:T(8,128)(2,1)S(1)}, u32[]{:S(2)}, u32[]{:S(2)}) collective-permute-start(bf16[256,1024]{1,0:T(8,128)(2,1)} %param.7), channel_id=1, source_target_pairs={{0,1},{1,0},{2,3},{3,2},{4,5},{5,4},{6,7},{7,6},{8,9},{9,8},{10,11... | collective-permute-start | bytes 1572872 | tf_op jit(solution)/shard_map/ppermute | solution.py:36
  3.7 3.0 %constant_dynamic-slice_fusion.3 = bf16[512,1792]{1,0:T(8,128)(2,1)} fusion(bf16[1024,3584]{1,0:T(8,128)(2,1)} %refs_5_.7, s32[]{:T(128)S(6)} %select_n.296), kind=kLoop, calls=%fused_computation.137 | loop fusion | bytes 3670020 | tf_op jit(solution)/shard_map/dynamic_slice | solution.py:140
  6.7 3.2 %constant_dynamic-slice_fusion.1 = bf16[512,1792]{1,0:T(8,128)(2,1)} fusion(bf16[1024,3584]{1,0:T(8,128)(2,1)} %refs_5_.7, s32[]{:T(128)S(6)} %select_n.296), kind=kLoop, calls=%fused_computation.131 | loop fusion | bytes 3670020 | tf_op jit(solution)/shard_map/dynamic_slice | solution.py:140
  14.2 1.7 %collective-permute-done = bf16[256,1024]{1,0:T(8,128)(2,1)S(1)} collective-permute-done((bf16[256,1024]{1,0:T(8,128)(2,1)}, bf16[256,1024]{1,0:T(8,128)(2,1)S(1)}, u32[]{:S(2)}, u32[]{:S(2)}) %collective-permute-start) | collective-permute-done | bytes 524320 | tf_op jit(solution)/shard_map/ppermute | solution.py:36
  16.4 3.5 %collective-permute-done.1.refs_3_.refs_4_ = bf16[320,1024]{1,0:T(8,128)(2,1)S(1)} collective-permute-done((bf16[320,1024]{1,0:T(8,128)(2,1)S(1)}, bf16[320,1024]{1,0:T(8,128)(2,1)S(1)}, u32[]{:S(2)}, u32[]{:S(2)}) %collective-permute-start.1) | collective-permute-done | bytes 655392 | tf_op jit(solution)/shard_map/ppermute | solution.py:36
  19.9 2.5 %collective-permute-start.10 = (bf16[240,1024]{1,0:T(8,128)(2,1)S(1)}, bf16[240,1024]{1,0:T(8,128)(2,1)S(1)}, u32[]{:S(2)}, u32[]{:S(2)}) collective-permute-start(bf16[240,1024]{1,0:T(8,128)(2,1)S(1)} %slice.216), channel_id=1, source_target_pairs={{0,3},{1,2},{2,1},{3,0},{4,7},{5,6},{6,5},{7,4},{8,11},{9,10},{10,... | collective-permute-start | bytes 1474568 | tf_op jit(solution)/shard_map/ppermute | solution.py:36
  22.4 6.4 %in_products.4 = f32[2,160,1792]{2,1,0:T(8,128)S(1)} custom-call(s32[1]{0:T(128)} %bitcast.refs_0_, bf16[320,1024]{1,0:T(8,128)(2,1)S(1)} %fusion.refs_1_.refs_2_, bf16[320,1024]{1,0:T(8,128)(2,1)S(1)} %fusion.refs_1_.refs_2_, bf16[320,1024]{1,0:T(8,128)(2,1)S(1)} %collective-permute-done.1.refs_3_.refs_4_, ...), custom_call_target="tpu_custom_call" | custom-call | tf_op jit(solution)/shard_map/in_products/pallas_call | solution.py:72
  29.1 1.6 collective-permute-start.6
  33.2 6.4 %in_products.5 = f32[2,160,1792]{2,1,0:T(8,128)S(1)} custom-call(s32[1]{0:T(128)} %bitcast.refs_0_, bf16[320,1024]{1,0:T(8,128)(2,1)S(1)} %fusion.refs_1_.refs_2_, bf16[320,1024]{1,0:T(8,128)(2,1)S(1)} %fusion.refs_1_.refs_2_, bf16[320,1024]{1,0:T(8,128)(2,1)S(1)} %collective-permute-done.1.refs_3_.refs_4_, ...), custom_call_target="tpu_custom_call" | custom-call | tf_op jit(solution)/shard_map/in_products/pallas_call | solution.py:72
  39.6 2.3 %collective-permute-done.8 = f16[80,1792]{1,0:T(8,128)(2,1)S(1)} collective-permute-done((f16[80,1792]{1,0:T(8,128)(2,1)S(1)}, f16[80,1792]{1,0:T(8,128)(2,1)S(1)}, u32[]{:S(2)}, u32[]{:S(2)}) %collective-permute-start.8) | collective-permute-done | bytes 286752 | tf_op jit(solution)/shard_map/ppermute | solution.py:42
  41.9 3.1 %collective-permute-done.9 = f16[80,1792]{1,0:T(8,128)(2,1)S(1)} collective-permute-done((f16[80,1792]{1,0:T(8,128)(2,1)S(1)}, f16[80,1792]{1,0:T(8,128)(2,1)S(1)}, u32[]{:S(2)}, u32[]{:S(2)}) %collective-permute-start.9) | collective-permute-done | bytes 286752 | tf_op jit(solution)/shard_map/ppermute | solution.py:42
  45.5 1.6 collective-permute-start.11
  47.1 1.9 %collective-permute-done.12.refs_3_.refs_4_ = bf16[240,1024]{1,0:T(8,128)(2,1)S(1)} collective-permute-done((bf16[240,1024]{1,0:T(8,128)(2,1)S(1)}, bf16[240,1024]{1,0:T(8,128)(2,1)S(1)}, u32[]{:S(2)}, u32[]{:S(2)}) %collective-permute-start.12) | collective-permute-done | bytes 491552 | tf_op jit(solution)/shard_map/ppermute | solution.py:36
  48.9 6.4 %in_products.6 = f32[2,160,1792]{2,1,0:T(8,128)S(1)} custom-call(s32[1]{0:T(128)} %bitcast.refs_0_, bf16[240,1024]{1,0:T(8,128)(2,1)S(1)} %collective-permute-done.10.refs_1_.refs_2_, bf16[240,1024]{1,0:T(8,128)(2,1)S(1)} %collective-permute-done.10.refs_1_.refs_2_, bf16[240,1024]{1,0:T(8,128)(2,1)S(1)} %collective-permute-done.12.refs_3_.refs_4_, ...), custom_call_target="tpu_custom_call" | custom-call | tf_op jit(solution)/shard_map/in_products/pallas_call | solution.py:72
  61.1 3.9 %collective-permute-done.14.refs_1_ = bf16[80,1024]{1,0:T(8,128)(2,1)S(1)} collective-permute-done((bf16[80,1024]{1,0:T(8,128)(2,1)S(1)}, bf16[80,1024]{1,0:T(8,128)(2,1)S(1)}, u32[]{:S(2)}, u32[]{:S(2)}) %collective-permute-start.14) | collective-permute-done | bytes 163872 | tf_op jit(solution)/shard_map/ppermute | solution.py:36
  69.0 6.5 %in_products.7 = f32[2,160,1792]{2,1,0:T(8,128)S(1)} custom-call(s32[1]{0:T(128)} %bitcast.refs_0_, bf16[80,1024]{1,0:T(8,128)(2,1)S(1)} %collective-permute-done.14.refs_1_, bf16[240,1024]{1,0:T(8,128)(2,1)S(1)} %collective-permute-done.10.refs_1_.refs_2_, bf16[80,1024]{1,0:T(8,128)(2,1)S(1)} %collective-permute-done.16.refs_3_, ...), custom_call_target="tpu_custom_call" | custom-call | tf_op jit(solution)/shard_map/in_products/pallas_call | solution.py:72
  75.5 6.4 %collective-permute-done.15 = bf16[160,1792]{1,0:T(8,128)(2,1)} collective-permute-done((bf16[160,1792]{1,0:T(8,128)(2,1)}, bf16[160,1792]{1,0:T(8,128)(2,1)}, u32[]{:S(2)}, u32[]{:S(2)}) %collective-permute-start.15) | collective-permute-done | bytes 573472 | tf_op jit(solution)/shard_map/ppermute | solution.py:42
  90.6 2.1 %fusion.6 = bf16[160,1024]{1,0:T(8,128)(2,1)} fusion(f32[160,1024]{1,0:T(8,128)S(1)} %fusion.33, bf16[3584,1024]{1,0:T(8,128)(2,1)S(1)} %bitcast.68, f32[]{:T(128)S(6)} %select_n.317, bf16[160,1792]{1,0:T(8,128)(2,1)S(1)} %get-tuple-element.170, bf16[160,1792]{1,0:T(8,128)(2,1)S(1)} %get-tuple-element.168), kind=kOutput, calls=%fused_computation.11 | convolution fusion | flops 1177190400 | bytes 9469956 | tf_op jit(solution)/shard_map/dot_general | solution.py:32
  98.0 2.6 %collective-permute-done.21 = bf16[80,1792]{1,0:T(8,128)(2,1)S(1)} collective-permute-done((bf16[80,1792]{1,0:T(8,128)(2,1)S(1)}, bf16[80,1792]{1,0:T(8,128)(2,1)S(1)}, u32[]{:S(2)}, u32[]{:S(2)}) %collective-permute-start.21) | collective-permute-done | bytes 286752 | tf_op jit(solution)/shard_map/ppermute | solution.py:42
  100.7 1.6 collective-permute-start.22
  103.7 6.8 %collective-permute-done.22 = bf16[160,1792]{1,0:T(8,128)(2,1)} collective-permute-done((bf16[160,1792]{1,0:T(8,128)(2,1)S(1)}, bf16[160,1792]{1,0:T(8,128)(2,1)}, u32[]{:S(2)}, u32[]{:S(2)}) %collective-permute-start.22) | collective-permute-done | bytes 573472 | tf_op jit(solution)/shard_map/ppermute | solution.py:42
  111.7 2.5 %collective-permute-start.27 = (bf16[160,1024]{1,0:T(8,128)(2,1)S(1)}, bf16[160,1024]{1,0:T(8,128)(2,1)S(1)}, u32[]{:S(2)}, u32[]{:S(2)}) collective-permute-start(bf16[160,1024]{1,0:T(8,128)(2,1)S(1)} %add_convert_fusion), channel_id=1, source_target_pairs={{0,3},{1,2},{2,1},{3,0},{4,7},{5,6},{6,5},{7,4},{8,11},{9,10},{10,... | collective-permute-start | bytes 983048 | tf_op jit(solution)/shard_map/ppermute | solution.py:36
  120.6 1.7 fusion.35
  124.0 6.7 %collective-permute-done.26 = bf16[160,1024]{1,0:T(8,128)(2,1)S(1)} collective-permute-done((bf16[160,1024]{1,0:T(8,128)(2,1)S(1)}, bf16[160,1024]{1,0:T(8,128)(2,1)S(1)}, u32[]{:S(2)}, u32[]{:S(2)}) %collective-permute-start.26) | collective-permute-done | bytes 327712 | tf_op jit(solution)/shard_map/ppermute | solution.py:36
  131.0 2.5 %collective-permute-start.29 = (bf16[160,1024]{1,0:T(8,128)(2,1)S(1)}, bf16[160,1024]{1,0:T(8,128)(2,1)S(1)}, u32[]{:S(2)}, u32[]{:S(2)}) collective-permute-start(bf16[160,1024]{1,0:T(8,128)(2,1)S(1)} %get-tuple-element.146.refs_6_), channel_id=1, source_target_pairs={{0,3},{1,2},{2,1},{3,0},{4,7},{5,6},{6,5},{7,4},{8,11},{9,10},{10,... | collective-permute-start | bytes 983048 | tf_op jit(solution)/shard_map/ppermute | solution.py:36
  135.0 1.6 collective-permute-start.28
  139.3 4.2 %collective-permute-done.29.refs_4_ = bf16[160,1024]{1,0:T(8,128)(2,1)S(1)} collective-permute-done((bf16[160,1024]{1,0:T(8,128)(2,1)S(1)}, bf16[160,1024]{1,0:T(8,128)(2,1)S(1)}, u32[]{:S(2)}, u32[]{:S(2)}) %collective-permute-start.29) | collective-permute-done | bytes 327712 | tf_op jit(solution)/shard_map/ppermute | solution.py:36
  143.5 4.5 %collective-permute-start.30 = (bf16[160,1024]{1,0:T(8,128)(2,1)S(1)}, bf16[160,1024]{1,0:T(8,128)(2,1)S(1)}, u32[]{:S(2)}, u32[]{:S(2)}) collective-permute-start(bf16[160,1024]{1,0:T(8,128)(2,1)S(1)} %collective-permute-done.29.refs_4_), channel_id=1, source_target_pairs={{0,1},{1,0},{2,3},{3,2},{4,5},{5,4},{6,7},{7,6},{8,9},{9,8},{10,11... | collective-permute-start | bytes 983048 | tf_op jit(solution)/shard_map/ppermute | solution.py:36
  149.6 2.1 %collective-permute-done.31 = f32[8,128]{1,0:T(8,128)S(1)} collective-permute-done((f32[8,128]{1,0:T(8,128)S(1)}, f32[8,128]{1,0:T(8,128)S(1)}, u32[]{:S(2)}, u32[]{:S(2)}) %collective-permute-start.31) | collective-permute-done | bytes 4128 | tf_op jit(solution)/shard_map/ppermute | solution.py:36
  153.6 2.3 %collective-permute-start.35 = (f32[8,128]{1,0:T(8,128)S(1)}, f32[8,128]{1,0:T(8,128)S(1)}, u32[]{:S(2)}, u32[]{:S(2)}) collective-permute-start(f32[8,128]{1,0:T(8,128)S(1)} %add.226), channel_id=1, source_target_pairs={{0,2},{1,3},{2,0},{3,1},{4,6},{5,7},{6,4},{7,5},{8,10},{9,11},{10,... | collective-permute-start | bytes 12296 | tf_op jit(solution)/shard_map/ppermute | solution.py:36
  155.9 2.1 %collective-permute-start.36 = (f32[8,128]{1,0:T(8,128)S(1)}, f32[8,128]{1,0:T(8,128)S(1)}, u32[]{:S(2)}, u32[]{:S(2)}) collective-permute-start(f32[8,128]{1,0:T(8,128)S(1)} %add.226), channel_id=1, source_target_pairs={{0,3},{1,2},{2,1},{3,0},{4,7},{5,6},{6,5},{7,4},{8,11},{9,10},{10,... | collective-permute-start | bytes 12296 | tf_op jit(solution)/shard_map/ppermute | solution.py:36
  158.8 10.7 %grad_products.1 = f32[3584,1024]{1,0:T(8,128)} custom-call(bf16[160,3584]{1,0:T(8,128)(2,1)} %copy-done.1, bf16[160,3584]{1,0:T(8,128)(2,1)} %pad_maximum_fusion.1.refs_1_, bf16[160,3584]{1,0:T(8,128)(2,1)} %copy-done.2, bf16[160,3584]{1,0:T(8,128)(2,1)} %pad_maximum_fusion.3.refs_3_, bf16[160,1024]{1,0:T(8,128)(2,1)} %copy-done.9, ...), custom_call_target="tpu_custom_call" | custom-call | tf_op jit(solution)/shard_map/grad_products/pallas_call | solution.py:103
  (159 shorter events, 50.8 us)
Async XLA Ops:
  0.6 15.2 %collective-permute-start = (bf16[256,1024]{1,0:T(8,128)(2,1)}, bf16[256,1024]{1,0:T(8,128)(2,1)S(1)}, u32[]{:S(2)}, u32[]{:S(2)}) collective-permute-start(bf16[256,1024]{1,0:T(8,128)(2,1)} %param.7), channel_id=1, source_target_pairs={{0,1},{1,0},{2,3},{3,2},{4,5},{5,4},{6,7},{7,6},{8,9},{9,8},{10,11... | collective-permute-start | bytes 1572872 | tf_op jit(solution)/shard_map/ppermute | solution.py:36
  6.7 15.6 %collective-permute-start.2 = (bf16[512,1792]{1,0:T(8,128)(2,1)}, bf16[512,1792]{1,0:T(8,128)(2,1)S(1)}, u32[]{:S(2)}, u32[]{:S(2)}) collective-permute-start(bf16[512,1792]{1,0:T(8,128)(2,1)} %constant_dynamic-slice_fusion.3), channel_id=1, source_target_pairs={{0,4},{4,0},{8,12},{12,8},{16,20},{20,16},{24,28},{28,24},{1,5},{5... | collective-permute-start | bytes 5505032 | tf_op jit(solution)/shard_map/ppermute | solution.py:36
  9.9 12.5 %collective-permute-start.3 = (bf16[512,1792]{1,0:T(8,128)(2,1)}, bf16[512,1792]{1,0:T(8,128)(2,1)}, u32[]{:S(2)}, u32[]{:S(2)}) collective-permute-start(bf16[512,1792]{1,0:T(8,128)(2,1)} %constant_dynamic-slice_fusion.1), channel_id=1, source_target_pairs={{0,4},{4,0},{8,12},{12,8},{16,20},{20,16},{24,28},{28,24},{1,5},{5... | collective-permute-start | bytes 5505032 | tf_op jit(solution)/shard_map/ppermute | solution.py:36
  11.5 10.8 %collective-permute-start.4 = (bf16[512,1792]{1,0:T(8,128)(2,1)}, bf16[512,1792]{1,0:T(8,128)(2,1)}, u32[]{:S(2)}, u32[]{:S(2)}) collective-permute-start(bf16[512,1792]{1,0:T(8,128)(2,1)} %constant_dynamic-slice_fusion.2), channel_id=1, source_target_pairs={{0,4},{4,0},{8,12},{12,8},{16,20},{20,16},{24,28},{28,24},{1,5},{5... | collective-permute-start | bytes 5505032 | tf_op jit(solution)/shard_map/ppermute | solution.py:36
  13.2 9.2 %collective-permute-start.5 = (bf16[512,1792]{1,0:T(8,128)(2,1)}, bf16[512,1792]{1,0:T(8,128)(2,1)}, u32[]{:S(2)}, u32[]{:S(2)}) collective-permute-start(bf16[512,1792]{1,0:T(8,128)(2,1)} %constant_dynamic-slice_fusion), channel_id=1, source_target_pairs={{0,4},{4,0},{8,12},{12,8},{16,20},{20,16},{24,28},{28,24},{1,5},{5... | collective-permute-start | bytes 5505032 | tf_op jit(solution)/shard_map/ppermute | solution.py:36
  16.2 3.6 %collective-permute-start.1 = (bf16[320,1024]{1,0:T(8,128)(2,1)S(1)}, bf16[320,1024]{1,0:T(8,128)(2,1)S(1)}, u32[]{:S(2)}, u32[]{:S(2)}) collective-permute-start(bf16[320,1024]{1,0:T(8,128)(2,1)S(1)} %fusion.refs_1_.refs_2_), channel_id=1, source_target_pairs={{0,4},{4,0},{8,12},{12,8},{16,20},{20,16},{24,28},{28,24},{1,5},{5... | collective-permute-start | bytes 1966088 | tf_op jit(solution)/shard_map/ppermute | solution.py:36
  19.9 19.7 %collective-permute-start.10 = (bf16[240,1024]{1,0:T(8,128)(2,1)S(1)}, bf16[240,1024]{1,0:T(8,128)(2,1)S(1)}, u32[]{:S(2)}, u32[]{:S(2)}) collective-permute-start(bf16[240,1024]{1,0:T(8,128)(2,1)S(1)} %slice.216), channel_id=1, source_target_pairs={{0,3},{1,2},{2,1},{3,0},{4,7},{5,6},{6,5},{7,4},{8,11},{9,10},{10,... | collective-permute-start | bytes 1474568 | tf_op jit(solution)/shard_map/ppermute | solution.py:36
  29.1 10.5 %collective-permute-start.6 = (f16[80,1792]{1,0:T(8,128)(2,1)S(1)}, f16[80,1792]{1,0:T(8,128)(2,1)S(1)}, u32[]{:S(2)}, u32[]{:S(2)}) collective-permute-start(f16[80,1792]{1,0:T(8,128)(2,1)S(1)} %get-tuple-element.191), channel_id=1, source_target_pairs={{0,8},{4,20},{8,0},{12,28},{16,24},{20,4},{24,16},{28,12},{1,9},{5... | collective-permute-start | bytes 860168 | tf_op jit(solution)/shard_map/ppermute | solution.py:42
  30.6 9.0 %collective-permute-start.7 = (f16[80,1792]{1,0:T(8,128)(2,1)S(1)}, f16[80,1792]{1,0:T(8,128)(2,1)S(1)}, u32[]{:S(2)}, u32[]{:S(2)}) collective-permute-start(f16[80,1792]{1,0:T(8,128)(2,1)S(1)} %get-tuple-element.190), channel_id=1, source_target_pairs={{0,8},{4,20},{8,0},{12,28},{16,24},{20,4},{24,16},{28,12},{1,9},{5... | collective-permute-start | bytes 860168 | tf_op jit(solution)/shard_map/ppermute | solution.py:42
  31.2 10.8 %collective-permute-start.8 = (f16[80,1792]{1,0:T(8,128)(2,1)S(1)}, f16[80,1792]{1,0:T(8,128)(2,1)S(1)}, u32[]{:S(2)}, u32[]{:S(2)}) collective-permute-start(f16[80,1792]{1,0:T(8,128)(2,1)S(1)} %get-tuple-element.189), channel_id=1, source_target_pairs={{0,8},{4,20},{8,0},{12,28},{16,24},{20,4},{24,16},{28,12},{1,9},{5... | collective-permute-start | bytes 860168 | tf_op jit(solution)/shard_map/ppermute | solution.py:42
  32.7 12.3 %collective-permute-start.9 = (f16[80,1792]{1,0:T(8,128)(2,1)S(1)}, f16[80,1792]{1,0:T(8,128)(2,1)S(1)}, u32[]{:S(2)}, u32[]{:S(2)}) collective-permute-start(f16[80,1792]{1,0:T(8,128)(2,1)S(1)} %get-tuple-element.188), channel_id=1, source_target_pairs={{0,8},{4,20},{8,0},{12,28},{16,24},{20,4},{24,16},{28,12},{1,9},{5... | collective-permute-start | bytes 860168 | tf_op jit(solution)/shard_map/ppermute | solution.py:42
  45.5 9.8 %collective-permute-start.11 = (f16[160,1792]{1,0:T(8,128)(2,1)S(1)}, f16[160,1792]{1,0:T(8,128)(2,1)S(1)}, u32[]{:S(2)}, u32[]{:S(2)}) collective-permute-start(f16[160,1792]{1,0:T(8,128)(2,1)S(1)} %pad_maximum_fusion.4), channel_id=1, source_target_pairs={{0,16},{4,12},{8,24},{12,4},{16,0},{20,28},{24,8},{28,20},{1,17},{... | collective-permute-start | bytes 1720328 | tf_op jit(solution)/shard_map/ppermute | solution.py:42
  55.6 9.5 %collective-permute-start.13 = (bf16[80,1792]{1,0:T(8,128)(2,1)S(1)}, bf16[80,1792]{1,0:T(8,128)(2,1)S(1)}, u32[]{:S(2)}, u32[]{:S(2)}) collective-permute-start(bf16[80,1792]{1,0:T(8,128)(2,1)S(1)} %multiply_convert_fusion.2), channel_id=1, source_target_pairs={{0,16},{4,12},{8,24},{12,4},{16,0},{20,28},{24,8},{28,20},{1,17},{... | collective-permute-start | bytes 860168 | tf_op jit(solution)/shard_map/ppermute | solution.py:42
  57.1 8.0 %collective-permute-start.14 = (bf16[80,1024]{1,0:T(8,128)(2,1)S(1)}, bf16[80,1024]{1,0:T(8,128)(2,1)S(1)}, u32[]{:S(2)}, u32[]{:S(2)}) collective-permute-start(bf16[80,1024]{1,0:T(8,128)(2,1)S(1)} %slice.217), channel_id=1, source_target_pairs={{0,3},{1,2},{2,1},{3,0},{4,7},{5,6},{6,5},{7,4},{8,11},{9,10},{10,... | collective-permute-start | bytes 491528 | tf_op jit(solution)/shard_map/ppermute | solution.py:36
  59.6 22.3 %collective-permute-start.19 = (f16[2,160,1792]{2,1,0:T(8,128)(2,1)}, f16[2,160,1792]{2,1,0:T(8,128)(2,1)}, u32[]{:S(2)}, u32[]{:S(2)}) collective-permute-start(f16[2,160,1792]{2,1,0:T(8,128)(2,1)} %convert_element_type.107), channel_id=1, source_target_pairs={{0,8},{4,20},{8,0},{12,28},{16,24},{20,4},{24,16},{28,12},{1,9},{5... | collective-permute-start | bytes 3440648 | tf_op jit(solution)/shard_map/ppermute | solution.py:42
  66.6 15.3 %collective-permute-start.15 = (bf16[160,1792]{1,0:T(8,128)(2,1)}, bf16[160,1792]{1,0:T(8,128)(2,1)}, u32[]{:S(2)}, u32[]{:S(2)}) collective-permute-start(bf16[160,1792]{1,0:T(8,128)(2,1)} %constant_dynamic-update-slice_fusion), channel_id=1, source_target_pairs={{0,8},{4,20},{8,0},{12,28},{16,24},{20,4},{24,16},{28,12},{1,9},{5... | collective-permute-start | bytes 1720328 | tf_op jit(solution)/shard_map/ppermute | solution.py:42
  67.4 17.1 %collective-permute-start.17 = (bf16[160,1792]{1,0:T(8,128)(2,1)}, bf16[160,1792]{1,0:T(8,128)(2,1)S(1)}, u32[]{:S(2)}, u32[]{:S(2)}) collective-permute-start(bf16[160,1792]{1,0:T(8,128)(2,1)} %constant_dynamic-update-slice_fusion), channel_id=1, source_target_pairs={{0,4},{4,0},{8,12},{12,8},{16,20},{20,16},{24,28},{28,24},{1,5},{5... | collective-permute-start | bytes 1720328 | tf_op jit(solution)/shard_map/ppermute | solution.py:36
  83.9 9.8 %collective-permute-start.20 = (f16[160,1792]{1,0:T(8,128)(2,1)S(1)}, f16[160,1792]{1,0:T(8,128)(2,1)S(1)}, u32[]{:S(2)}, u32[]{:S(2)}) collective-permute-start(f16[160,1792]{1,0:T(8,128)(2,1)S(1)} %pad_maximum_fusion.5), channel_id=1, source_target_pairs={{0,16},{4,12},{8,24},{12,4},{16,0},{20,28},{24,8},{28,20},{1,17},{... | collective-permute-start | bytes 1720328 | tf_op jit(solution)/shard_map/ppermute | solution.py:42
  92.7 10.9 %collective-permute-start.23 = (bf16[160,1024]{1,0:T(8,128)(2,1)}, bf16[160,1024]{1,0:T(8,128)(2,1)S(1)}, u32[]{:S(2)}, u32[]{:S(2)}) collective-permute-start(bf16[160,1024]{1,0:T(8,128)(2,1)} %fusion.6), channel_id=1, source_target_pairs={{0,1},{1,0},{2,3},{3,2},{4,5},{5,4},{6,7},{7,6},{8,9},{9,8},{10,11... | collective-permute-start | bytes 983048 | tf_op jit(solution)/shard_map/ppermute | solution.py:36
  93.9 6.7 %collective-permute-start.21 = (bf16[80,1792]{1,0:T(8,128)(2,1)S(1)}, bf16[80,1792]{1,0:T(8,128)(2,1)S(1)}, u32[]{:S(2)}, u32[]{:S(2)}) collective-permute-start(bf16[80,1792]{1,0:T(8,128)(2,1)S(1)} %multiply_convert_fusion.1), channel_id=1, source_target_pairs={{0,16},{4,12},{8,24},{12,4},{16,0},{20,28},{24,8},{28,20},{1,17},{... | collective-permute-start | bytes 860168 | tf_op jit(solution)/shard_map/ppermute | solution.py:42
  100.7 9.9 %collective-permute-start.22 = (bf16[160,1792]{1,0:T(8,128)(2,1)S(1)}, bf16[160,1792]{1,0:T(8,128)(2,1)}, u32[]{:S(2)}, u32[]{:S(2)}) collective-permute-start(bf16[160,1792]{1,0:T(8,128)(2,1)S(1)} %constant_dynamic-update-slice_fusion.2), channel_id=1, source_target_pairs={{0,8},{4,20},{8,0},{12,28},{16,24},{20,4},{24,16},{28,12},{1,9},{5... | collective-permute-start | bytes 1720328 | tf_op jit(solution)/shard_map/ppermute | solution.py:42
  103.5 10.6 %collective-permute-start.24 = (bf16[160,1792]{1,0:T(8,128)(2,1)S(1)}, bf16[160,1792]{1,0:T(8,128)(2,1)S(1)}, u32[]{:S(2)}, u32[]{:S(2)}) collective-permute-start(bf16[160,1792]{1,0:T(8,128)(2,1)S(1)} %constant_dynamic-update-slice_fusion.2), channel_id=1, source_target_pairs={{0,4},{4,0},{8,12},{12,8},{16,20},{20,16},{24,28},{28,24},{1,5},{5... | collective-permute-start | bytes 1720328 | tf_op jit(solution)/shard_map/ppermute | solution.py:36
  110.5 3.6 %collective-permute-start.25 = (bf16[160,1792]{1,0:T(8,128)(2,1)}, bf16[160,1792]{1,0:T(8,128)(2,1)S(1)}, u32[]{:S(2)}, u32[]{:S(2)}) collective-permute-start(bf16[160,1792]{1,0:T(8,128)(2,1)} %collective-permute-done.22), channel_id=1, source_target_pairs={{0,4},{4,0},{8,12},{12,8},{16,20},{20,16},{24,28},{28,24},{1,5},{5... | collective-permute-start | bytes 1720328 | tf_op jit(solution)/shard_map/ppermute | solution.py:36
  111.7 12.3 %collective-permute-start.27 = (bf16[160,1024]{1,0:T(8,128)(2,1)S(1)}, bf16[160,1024]{1,0:T(8,128)(2,1)S(1)}, u32[]{:S(2)}, u32[]{:S(2)}) collective-permute-start(bf16[160,1024]{1,0:T(8,128)(2,1)S(1)} %add_convert_fusion), channel_id=1, source_target_pairs={{0,3},{1,2},{2,1},{3,0},{4,7},{5,6},{6,5},{7,4},{8,11},{9,10},{10,... | collective-permute-start | bytes 983048 | tf_op jit(solution)/shard_map/ppermute | solution.py:36
  120.2 10.5 %collective-permute-start.26 = (bf16[160,1024]{1,0:T(8,128)(2,1)S(1)}, bf16[160,1024]{1,0:T(8,128)(2,1)S(1)}, u32[]{:S(2)}, u32[]{:S(2)}) collective-permute-start(bf16[160,1024]{1,0:T(8,128)(2,1)S(1)} %fusion.5), channel_id=1, source_target_pairs={{0,1},{1,0},{2,3},{3,2},{4,5},{5,4},{6,7},{7,6},{8,9},{9,8},{10,11... | collective-permute-start | bytes 983048 | tf_op jit(solution)/shard_map/ppermute | solution.py:36
  131.0 12.5 %collective-permute-start.29 = (bf16[160,1024]{1,0:T(8,128)(2,1)S(1)}, bf16[160,1024]{1,0:T(8,128)(2,1)S(1)}, u32[]{:S(2)}, u32[]{:S(2)}) collective-permute-start(bf16[160,1024]{1,0:T(8,128)(2,1)S(1)} %get-tuple-element.146.refs_6_), channel_id=1, source_target_pairs={{0,3},{1,2},{2,1},{3,0},{4,7},{5,6},{6,5},{7,4},{8,11},{9,10},{10,... | collective-permute-start | bytes 983048 | tf_op jit(solution)/shard_map/ppermute | solution.py:36
  133.6 16.0 %collective-permute-start.32 = (bf16[160,1024]{1,0:T(8,128)(2,1)S(1)}, bf16[160,1024]{1,0:T(8,128)(2,1)S(1)}, u32[]{:S(2)}, u32[]{:S(2)}) collective-permute-start(bf16[160,1024]{1,0:T(8,128)(2,1)S(1)} %get-tuple-element.146.refs_6_), channel_id=1, source_target_pairs={{0,1},{1,0},{2,3},{3,2},{4,5},{5,4},{6,7},{7,6},{8,9},{9,8},{10,11... | collective-permute-start | bytes 983048 | tf_op jit(solution)/shard_map/ppermute | solution.py:36
  135.0 3.7 %collective-permute-start.28 = (f32[8,128]{1,0:T(8,128)S(1)}, f32[8,128]{1,0:T(8,128)S(1)}, u32[]{:S(2)}, u32[]{:S(2)}) collective-permute-start(f32[8,128]{1,0:T(8,128)S(1)} %broadcast_in_dim.58), channel_id=1, source_target_pairs={{0,8},{4,12},{8,0},{12,4},{16,24},{20,28},{24,16},{28,20},{1,9},{5... | collective-permute-start | bytes 12296 | tf_op jit(solution)/shard_map/ppermute | solution.py:36
  143.5 14.6 %collective-permute-start.30 = (bf16[160,1024]{1,0:T(8,128)(2,1)S(1)}, bf16[160,1024]{1,0:T(8,128)(2,1)S(1)}, u32[]{:S(2)}, u32[]{:S(2)}) collective-permute-start(bf16[160,1024]{1,0:T(8,128)(2,1)S(1)} %collective-permute-done.29.refs_4_), channel_id=1, source_target_pairs={{0,1},{1,0},{2,3},{3,2},{4,5},{5,4},{6,7},{7,6},{8,9},{9,8},{10,11... | collective-permute-start | bytes 983048 | tf_op jit(solution)/shard_map/ppermute | solution.py:36
  153.6 16.0 %collective-permute-start.34 = (f32[8,128]{1,0:T(8,128)S(1)}, f32[8,128]{1,0:T(8,128)S(1)}, u32[]{:S(2)}, u32[]{:S(2)}) collective-permute-start(f32[8,128]{1,0:T(8,128)S(1)} %add.226), channel_id=1, source_target_pairs={{0,1},{1,0},{2,3},{3,2},{4,5},{5,4},{6,7},{7,6},{8,9},{9,8},{10,11... | collective-permute-start | bytes 12296 | tf_op jit(solution)/shard_map/ppermute | solution.py:36
  153.6 16.0 %collective-permute-start.35 = (f32[8,128]{1,0:T(8,128)S(1)}, f32[8,128]{1,0:T(8,128)S(1)}, u32[]{:S(2)}, u32[]{:S(2)}) collective-permute-start(f32[8,128]{1,0:T(8,128)S(1)} %add.226), channel_id=1, source_target_pairs={{0,2},{1,3},{2,0},{3,1},{4,6},{5,7},{6,4},{7,5},{8,10},{9,11},{10,... | collective-permute-start | bytes 12296 | tf_op jit(solution)/shard_map/ppermute | solution.py:36
  155.9 13.7 %collective-permute-start.36 = (f32[8,128]{1,0:T(8,128)S(1)}, f32[8,128]{1,0:T(8,128)S(1)}, u32[]{:S(2)}, u32[]{:S(2)}) collective-permute-start(f32[8,128]{1,0:T(8,128)S(1)} %add.226), channel_id=1, source_target_pairs={{0,3},{1,2},{2,1},{3,0},{4,7},{5,6},{6,5},{7,4},{8,11},{9,10},{10,... | collective-permute-start | bytes 12296 | tf_op jit(solution)/shard_map/ppermute | solution.py:36
  (27 other events, 124.8 us)
where the time goes:
time: 170 us
  waiting for transfers between devices  50.1 us (29%)
  starting transfers between devices  38.1 us (22%)
  Pallas kernels  36.4 us (21%)
  local copies, waits for them, and re-layouts  16.9 us (10%)
  other arithmetic  13.6 us (8%)
  matrix products  13 us (8%)
  between operations  1.98 us (1%)
    ppermute x26, waiting for transfers between devices, swap(): lax.ppermute(x, axis, [(i, i ^ bit) for i in range(lax.axis_size(axis))])  28.6 us
    pallas_call x4, Pallas kernels, in_products(): pl.pallas_call(lambda *refs: in_kernel(*refs, scale=scale), grid_spec=plt...  25.7 us
    ppermute x26, starting transfers between devices, swap(): lax.ppermute(x, axis, [(i, i ^ bit) for i in range(lax.axis_size(axis))])  25.3 us
    ppermute x11, waiting for transfers between devices, by_core(): lax.ppermute(x, 'fsdp', [(i, i ^ (odd if i % 2 else even)) for i in range...  21.6 us
    dot_general x10, matrix products, dot(): return jnp.dot(a, b, preferred_element_type=f32)  13 us
    ppermute x11, starting transfers between devices, by_core(): lax.ppermute(x, 'fsdp', [(i, i ^ (odd if i % 2 else even)) for i in range...  12.8 us
    pallas_call x1, Pallas kernels, grad_products(): pl.pallas_call(grad_kernel, grid=(steps,), in_specs=specs, out_specs=pl.B...  10.7 us
    dynamic_slice x4, local copies, waits for them, and re-layouts, traded(): sent.append(lax.dynamic_slice(after(w, *sent[-1:]), at, (depth, half)))  8.93 us
  transfers between devices with their start and end apart: 37, of which 18 were waited for; matrix products, arithmetic and copies ran while one was open for 22% of the time, Pallas kernels for 21%

commit v1 on v0

--- a/solution.py
+++ b/solution.py
@@ -107,7 +107,6 @@
         out_specs=pl.BlockSpec((tile, cols), lambda j: (j, 0)),
         out_shape=jax.ShapeDtypeStruct((width, cols), f32),
         compiler_params=pltpu.CompilerParams(vmem_limit_bytes=GRAD_VMEM_BYTES),
-        cost_estimate=FREE,
         name="grad_products",
     )(*hiddens, *deltas)
 
@@ -319,6 +318,8 @@
     b.gather_whole()
     b.down(frozen_b)
     b.down_rest()
+    a.parts = list(go(*a.parts))
+    did(a.parts[0])
     b.delta(a.far)
     value = jnp.full((8, 128), b.loss, f32)
     value = did(value + go(swap("fsdp", 2, value)))

time: 170 us -> 170 us (level)
  no operation moved by 1% of the time
where the time goes in v1:
time: 170 us
  waiting for transfers between devices  50.1 us (29%)
  starting transfers between devices  38.1 us (22%)
  Pallas kernels  36.4 us (21%)
  local copies, waits for them, and re-layouts  16.9 us (10%)
  other arithmetic  13.6 us (8%)
  matrix products  13 us (8%)
  between operations  1.98 us (1%)
    ppermute x26, waiting for transfers between devices, swap(): lax.ppermute(x, axis, [(i, i ^ bit) for i in range(lax.axis_size(axis))])  28.6 us
    pallas_call x4, Pallas kernels, in_products(): pl.pallas_call(lambda *refs: in_kernel(*refs, scale=scale), grid_spec=plt...  25.7 us
    ppermute x26, starting transfers between devices, swap(): lax.ppermute(x, axis, [(i, i ^ bit) for i in range(lax.axis_size(axis))])  25.3 us
    ppermute x11, waiting for transfers between devices, by_core(): lax.ppermute(x, 'fsdp', [(i, i ^ (odd if i % 2 else even)) for i in range...  21.6 us
    dot_general x10, matrix products, dot(): return jnp.dot(a, b, preferred_element_type=f32)  13 us
    ppermute x11, starting transfers between devices, by_core(): lax.ppermute(x, 'fsdp', [(i, i ^ (odd if i % 2 else even)) for i in range...  12.8 us
    pallas_call x1, Pallas kernels, grad_products(): pl.pallas_call(grad_kernel, grid=(steps,), in_specs=specs, out_specs=pl.B...  10.7 us
    dynamic_slice x4, local copies, waits for them, and re-layouts, traded(): sent.append(lax.dynamic_slice(after(w, *sent[-1:]), at, (depth, half)))  8.93 us
  transfers between devices with their start and end apart: 37, of which 18 were waited for; matrix products, arithmetic and copies ran while one was open for 22% of the time, Pallas kernels for 21%

profile of v1, /device:TPU:0, one launch (start us, length us, event | category | flops | bytes accessed | tf_op | source)
XLA Modules:
  0.0 170.1 jit_solution(18011515617499351154)
XLA Ops:
  0.6 3.1 %collective-permute-start = (bf16[256,1024]{1,0:T(8,128)(2,1)}, bf16[256,1024]{1,0:T(8,128)(2,1)S(1)}, u32[]{:S(2)}, u32[]{:S(2)}) collective-permute-start(bf16[256,1024]{1,0:T(8,128)(2,1)} %param.7), channel_id=1, source_target_pairs={{0,1},{1,0},{2,3},{3,2},{4,5},{5,4},{6,7},{7,6},{8,9},{9,8},{10,11... | collective-permute-start | bytes 1572872 | tf_op jit(solution)/shard_map/ppermute | solution.py:36
  3.7 3.0 %constant_dynamic-slice_fusion.3 = bf16[512,1792]{1,0:T(8,128)(2,1)} fusion(bf16[1024,3584]{1,0:T(8,128)(2,1)} %refs_5_.7, s32[]{:T(128)S(6)} %select_n.296), kind=kLoop, calls=%fused_computation.137 | loop fusion | bytes 3670020 | tf_op jit(solution)/shard_map/dynamic_slice | solution.py:139
  6.7 3.2 %constant_dynamic-slice_fusion.1 = bf16[512,1792]{1,0:T(8,128)(2,1)} fusion(bf16[1024,3584]{1,0:T(8,128)(2,1)} %refs_5_.7, s32[]{:T(128)S(6)} %select_n.296), kind=kLoop, calls=%fused_computation.131 | loop fusion | bytes 3670020 | tf_op jit(solution)/shard_map/dynamic_slice | solution.py:139
  14.2 1.7 %collective-permute-done = bf16[256,1024]{1,0:T(8,128)(2,1)S(1)} collective-permute-done((bf16[256,1024]{1,0:T(8,128)(2,1)}, bf16[256,1024]{1,0:T(8,128)(2,1)S(1)}, u32[]{:S(2)}, u32[]{:S(2)}) %collective-permute-start) | collective-permute-done | bytes 524320 | tf_op jit(solution)/shard_map/ppermute | solution.py:36
  16.4 3.5 %collective-permute-done.1.refs_3_.refs_4_ = bf16[320,1024]{1,0:T(8,128)(2,1)S(1)} collective-permute-done((bf16[320,1024]{1,0:T(8,128)(2,1)S(1)}, bf16[320,1024]{1,0:T(8,128)(2,1)S(1)}, u32[]{:S(2)}, u32[]{:S(2)}) %collective-permute-start.1) | collective-permute-done | bytes 655392 | tf_op jit(solution)/shard_map/ppermute | solution.py:36
  19.9 2.5 %collective-permute-start.10 = (bf16[240,1024]{1,0:T(8,128)(2,1)S(1)}, bf16[240,1024]{1,0:T(8,128)(2,1)S(1)}, u32[]{:S(2)}, u32[]{:S(2)}) collective-permute-start(bf16[240,1024]{1,0:T(8,128)(2,1)S(1)} %slice.216), channel_id=1, source_target_pairs={{0,3},{1,2},{2,1},{3,0},{4,7},{5,6},{6,5},{7,4},{8,11},{9,10},{10,... | collective-permute-start | bytes 1474568 | tf_op jit(solution)/shard_map/ppermute | solution.py:36
  22.4 6.4 %in_products.4 = f32[2,160,1792]{2,1,0:T(8,128)S(1)} custom-call(s32[1]{0:T(128)} %bitcast.refs_0_, bf16[320,1024]{1,0:T(8,128)(2,1)S(1)} %fusion.refs_1_.refs_2_, bf16[320,1024]{1,0:T(8,128)(2,1)S(1)} %fusion.refs_1_.refs_2_, bf16[320,1024]{1,0:T(8,128)(2,1)S(1)} %collective-permute-done.1.refs_3_.refs_4_, ...), custom_call_target="tpu_custom_call" | custom-call | tf_op jit(solution)/shard_map/in_products/pallas_call | solution.py:72
  29.1 1.6 collective-permute-start.6
  33.2 6.4 %in_products.5 = f32[2,160,1792]{2,1,0:T(8,128)S(1)} custom-call(s32[1]{0:T(128)} %bitcast.refs_0_, bf16[320,1024]{1,0:T(8,128)(2,1)S(1)} %fusion.refs_1_.refs_2_, bf16[320,1024]{1,0:T(8,128)(2,1)S(1)} %fusion.refs_1_.refs_2_, bf16[320,1024]{1,0:T(8,128)(2,1)S(1)} %collective-permute-done.1.refs_3_.refs_4_, ...), custom_call_target="tpu_custom_call" | custom-call | tf_op jit(solution)/shard_map/in_products/pallas_call | solution.py:72
  39.6 2.3 %collective-permute-done.8 = f16[80,1792]{1,0:T(8,128)(2,1)S(1)} collective-permute-done((f16[80,1792]{1,0:T(8,128)(2,1)S(1)}, f16[80,1792]{1,0:T(8,128)(2,1)S(1)}, u32[]{:S(2)}, u32[]{:S(2)}) %collective-permute-start.8) | collective-permute-done | bytes 286752 | tf_op jit(solution)/shard_map/ppermute | solution.py:42
  41.9 3.1 %collective-permute-done.9 = f16[80,1792]{1,0:T(8,128)(2,1)S(1)} collective-permute-done((f16[80,1792]{1,0:T(8,128)(2,1)S(1)}, f16[80,1792]{1,0:T(8,128)(2,1)S(1)}, u32[]{:S(2)}, u32[]{:S(2)}) %collective-permute-start.9) | collective-permute-done | bytes 286752 | tf_op jit(solution)/shard_map/ppermute | solution.py:42
  45.5 1.6 collective-permute-start.11
  47.1 1.9 %collective-permute-done.12.refs_3_.refs_4_ = bf16[240,1024]{1,0:T(8,128)(2,1)S(1)} collective-permute-done((bf16[240,1024]{1,0:T(8,128)(2,1)S(1)}, bf16[240,1024]{1,0:T(8,128)(2,1)S(1)}, u32[]{:S(2)}, u32[]{:S(2)}) %collective-permute-start.12) | collective-permute-done | bytes 491552 | tf_op jit(solution)/shard_map/ppermute | solution.py:36
  48.9 6.4 %in_products.6 = f32[2,160,1792]{2,1,0:T(8,128)S(1)} custom-call(s32[1]{0:T(128)} %bitcast.refs_0_, bf16[240,1024]{1,0:T(8,128)(2,1)S(1)} %collective-permute-done.10.refs_1_.refs_2_, bf16[240,1024]{1,0:T(8,128)(2,1)S(1)} %collective-permute-done.10.refs_1_.refs_2_, bf16[240,1024]{1,0:T(8,128)(2,1)S(1)} %collective-permute-done.12.refs_3_.refs_4_, ...), custom_call_target="tpu_custom_call" | custom-call | tf_op jit(solution)/shard_map/in_products/pallas_call | solution.py:72
  61.1 3.9 %collective-permute-done.14.refs_1_ = bf16[80,1024]{1,0:T(8,128)(2,1)S(1)} collective-permute-done((bf16[80,1024]{1,0:T(8,128)(2,1)S(1)}, bf16[80,1024]{1,0:T(8,128)(2,1)S(1)}, u32[]{:S(2)}, u32[]{:S(2)}) %collective-permute-start.14) | collective-permute-done | bytes 163872 | tf_op jit(solution)/shard_map/ppermute | solution.py:36
  69.0 6.5 %in_products.7 = f32[2,160,1792]{2,1,0:T(8,128)S(1)} custom-call(s32[1]{0:T(128)} %bitcast.refs_0_, bf16[80,1024]{1,0:T(8,128)(2,1)S(1)} %collective-permute-done.14.refs_1_, bf16[240,1024]{1,0:T(8,128)(2,1)S(1)} %collective-permute-done.10.refs_1_.refs_2_, bf16[80,1024]{1,0:T(8,128)(2,1)S(1)} %collective-permute-done.16.refs_3_, ...), custom_call_target="tpu_custom_call" | custom-call | tf_op jit(solution)/shard_map/in_products/pallas_call | solution.py:72
  75.5 6.4 %collective-permute-done.15 = bf16[160,1792]{1,0:T(8,128)(2,1)} collective-permute-done((bf16[160,1792]{1,0:T(8,128)(2,1)}, bf16[160,1792]{1,0:T(8,128)(2,1)}, u32[]{:S(2)}, u32[]{:S(2)}) %collective-permute-start.15) | collective-permute-done | bytes 573472 | tf_op jit(solution)/shard_map/ppermute | solution.py:42
  90.6 2.1 %fusion.6 = bf16[160,1024]{1,0:T(8,128)(2,1)} fusion(f32[160,1024]{1,0:T(8,128)S(1)} %fusion.33, bf16[3584,1024]{1,0:T(8,128)(2,1)S(1)} %bitcast.68, f32[]{:T(128)S(6)} %select_n.317, bf16[160,1792]{1,0:T(8,128)(2,1)S(1)} %get-tuple-element.174, bf16[160,1792]{1,0:T(8,128)(2,1)S(1)} %get-tuple-element.172), kind=kOutput, calls=%fused_computation.11 | convolution fusion | flops 1177190400 | bytes 9469956 | tf_op jit(solution)/shard_map/dot_general | solution.py:32
  98.0 2.6 %collective-permute-done.21 = bf16[80,1792]{1,0:T(8,128)(2,1)S(1)} collective-permute-done((bf16[80,1792]{1,0:T(8,128)(2,1)S(1)}, bf16[80,1792]{1,0:T(8,128)(2,1)S(1)}, u32[]{:S(2)}, u32[]{:S(2)}) %collective-permute-start.21) | collective-permute-done | bytes 286752 | tf_op jit(solution)/shard_map/ppermute | solution.py:42
  100.7 1.6 collective-permute-start.22
  103.7 6.8 %collective-permute-done.22 = bf16[160,1792]{1,0:T(8,128)(2,1)} collective-permute-done((bf16[160,1792]{1,0:T(8,128)(2,1)S(1)}, bf16[160,1792]{1,0:T(8,128)(2,1)}, u32[]{:S(2)}, u32[]{:S(2)}) %collective-permute-start.22) | collective-permute-done | bytes 573472 | tf_op jit(solution)/shard_map/ppermute | solution.py:42
  111.7 2.5 %collective-permute-start.27 = (bf16[160,1024]{1,0:T(8,128)(2,1)S(1)}, bf16[160,1024]{1,0:T(8,128)(2,1)S(1)}, u32[]{:S(2)}, u32[]{:S(2)}) collective-permute-start(bf16[160,1024]{1,0:T(8,128)(2,1)S(1)} %add_convert_fusion), channel_id=1, source_target_pairs={{0,3},{1,2},{2,1},{3,0},{4,7},{5,6},{6,5},{7,4},{8,11},{9,10},{10,... | collective-permute-start | bytes 983048 | tf_op jit(solution)/shard_map/ppermute | solution.py:36
  120.6 1.7 fusion.35
  124.0 6.7 %collective-permute-done.26 = bf16[160,1024]{1,0:T(8,128)(2,1)S(1)} collective-permute-done((bf16[160,1024]{1,0:T(8,128)(2,1)S(1)}, bf16[160,1024]{1,0:T(8,128)(2,1)S(1)}, u32[]{:S(2)}, u32[]{:S(2)}) %collective-permute-start.26) | collective-permute-done | bytes 327712 | tf_op jit(solution)/shard_map/ppermute | solution.py:36
  131.0 2.5 %collective-permute-start.29 = (bf16[160,1024]{1,0:T(8,128)(2,1)S(1)}, bf16[160,1024]{1,0:T(8,128)(2,1)S(1)}, u32[]{:S(2)}, u32[]{:S(2)}) collective-permute-start(bf16[160,1024]{1,0:T(8,128)(2,1)S(1)} %get-tuple-element.150.refs_6_), channel_id=1, source_target_pairs={{0,3},{1,2},{2,1},{3,0},{4,7},{5,6},{6,5},{7,4},{8,11},{9,10},{10,... | collective-permute-start | bytes 983048 | tf_op jit(solution)/shard_map/ppermute | solution.py:36
  135.0 1.6 collective-permute-start.28
  139.3 4.2 %collective-permute-done.29.refs_4_ = bf16[160,1024]{1,0:T(8,128)(2,1)S(1)} collective-permute-done((bf16[160,1024]{1,0:T(8,128)(2,1)S(1)}, bf16[160,1024]{1,0:T(8,128)(2,1)S(1)}, u32[]{:S(2)}, u32[]{:S(2)}) %collective-permute-start.29) | collective-permute-done | bytes 327712 | tf_op jit(solution)/shard_map/ppermute | solution.py:36
  143.5 4.5 %collective-permute-start.30 = (bf16[160,1024]{1,0:T(8,128)(2,1)S(1)}, bf16[160,1024]{1,0:T(8,128)(2,1)S(1)}, u32[]{:S(2)}, u32[]{:S(2)}) collective-permute-start(bf16[160,1024]{1,0:T(8,128)(2,1)S(1)} %collective-permute-done.29.refs_4_), channel_id=1, source_target_pairs={{0,1},{1,0},{2,3},{3,2},{4,5},{5,4},{6,7},{7,6},{8,9},{9,8},{10,11... | collective-permute-start | bytes 983048 | tf_op jit(solution)/shard_map/ppermute | solution.py:36
  149.6 2.1 %collective-permute-done.31 = f32[8,128]{1,0:T(8,128)S(1)} collective-permute-done((f32[8,128]{1,0:T(8,128)S(1)}, f32[8,128]{1,0:T(8,128)S(1)}, u32[]{:S(2)}, u32[]{:S(2)}) %collective-permute-start.31) | collective-permute-done | bytes 4128 | tf_op jit(solution)/shard_map/ppermute | solution.py:36
  153.6 2.3 %collective-permute-start.35 = (f32[8,128]{1,0:T(8,128)S(1)}, f32[8,128]{1,0:T(8,128)S(1)}, u32[]{:S(2)}, u32[]{:S(2)}) collective-permute-start(f32[8,128]{1,0:T(8,128)S(1)} %add.226), channel_id=1, source_target_pairs={{0,2},{1,3},{2,0},{3,1},{4,6},{5,7},{6,4},{7,5},{8,10},{9,11},{10,... | collective-permute-start | bytes 12296 | tf_op jit(solution)/shard_map/ppermute | solution.py:36
  155.9 2.1 %collective-permute-start.36 = (f32[8,128]{1,0:T(8,128)S(1)}, f32[8,128]{1,0:T(8,128)S(1)}, u32[]{:S(2)}, u32[]{:S(2)}) collective-permute-start(f32[8,128]{1,0:T(8,128)S(1)} %add.226), channel_id=1, source_target_pairs={{0,3},{1,2},{2,1},{3,0},{4,7},{5,6},{6,5},{7,4},{8,11},{9,10},{10,... | collective-permute-start | bytes 12296 | tf_op jit(solution)/shard_map/ppermute | solution.py:36
  158.8 10.7 %grad_products.1 = f32[3584,1024]{1,0:T(8,128)} custom-call(bf16[160,3584]{1,0:T(8,128)(2,1)} %copy-done.1, bf16[160,3584]{1,0:T(8,128)(2,1)} %pad_maximum_fusion.1.refs_1_, bf16[160,3584]{1,0:T(8,128)(2,1)} %copy-done.2, bf16[160,3584]{1,0:T(8,128)(2,1)} %pad_maximum_fusion.3.refs_3_, bf16[160,1024]{1,0:T(8,128)(2,1)} %copy-done.9, ...), custom_call_target="tpu_custom_call" | custom-call | tf_op jit(solution)/shard_map/grad_products/pallas_call | solution.py:103
  (159 shorter events, 50.8 us)
Async XLA Ops:
  0.6 15.2 %collective-permute-start = (bf16[256,1024]{1,0:T(8,128)(2,1)}, bf16[256,1024]{1,0:T(8,128)(2,1)S(1)}, u32[]{:S(2)}, u32[]{:S(2)}) collective-permute-start(bf16[256,1024]{1,0:T(8,128)(2,1)} %param.7), channel_id=1, source_target_pairs={{0,1},{1,0},{2,3},{3,2},{4,5},{5,4},{6,7},{7,6},{8,9},{9,8},{10,11... | collective-permute-start | bytes 1572872 | tf_op jit(solution)/shard_map/ppermute | solution.py:36
  6.7 15.6 %collective-permute-start.2 = (bf16[512,1792]{1,0:T(8,128)(2,1)}, bf16[512,1792]{1,0:T(8,128)(2,1)S(1)}, u32[]{:S(2)}, u32[]{:S(2)}) collective-permute-start(bf16[512,1792]{1,0:T(8,128)(2,1)} %constant_dynamic-slice_fusion.3), channel_id=1, source_target_pairs={{0,4},{4,0},{8,12},{12,8},{16,20},{20,16},{24,28},{28,24},{1,5},{5... | collective-permute-start | bytes 5505032 | tf_op jit(solution)/shard_map/ppermute | solution.py:36
  9.9 12.5 %collective-permute-start.3 = (bf16[512,1792]{1,0:T(8,128)(2,1)}, bf16[512,1792]{1,0:T(8,128)(2,1)}, u32[]{:S(2)}, u32[]{:S(2)}) collective-permute-start(bf16[512,1792]{1,0:T(8,128)(2,1)} %constant_dynamic-slice_fusion.1), channel_id=1, source_target_pairs={{0,4},{4,0},{8,12},{12,8},{16,20},{20,16},{24,28},{28,24},{1,5},{5... | collective-permute-start | bytes 5505032 | tf_op jit(solution)/shard_map/ppermute | solution.py:36
  11.5 10.8 %collective-permute-start.4 = (bf16[512,1792]{1,0:T(8,128)(2,1)}, bf16[512,1792]{1,0:T(8,128)(2,1)}, u32[]{:S(2)}, u32[]{:S(2)}) collective-permute-start(bf16[512,1792]{1,0:T(8,128)(2,1)} %constant_dynamic-slice_fusion.2), channel_id=1, source_target_pairs={{0,4},{4,0},{8,12},{12,8},{16,20},{20,16},{24,28},{28,24},{1,5},{5... | collective-permute-start | bytes 5505032 | tf_op jit(solution)/shard_map/ppermute | solution.py:36
  13.2 9.2 %collective-permute-start.5 = (bf16[512,1792]{1,0:T(8,128)(2,1)}, bf16[512,1792]{1,0:T(8,128)(2,1)}, u32[]{:S(2)}, u32[]{:S(2)}) collective-permute-start(bf16[512,1792]{1,0:T(8,128)(2,1)} %constant_dynamic-slice_fusion), channel_id=1, source_target_pairs={{0,4},{4,0},{8,12},{12,8},{16,20},{20,16},{24,28},{28,24},{1,5},{5... | collective-permute-start | bytes 5505032 | tf_op jit(solution)/shard_map/ppermute | solution.py:36
  16.2 3.6 %collective-permute-start.1 = (bf16[320,1024]{1,0:T(8,128)(2,1)S(1)}, bf16[320,1024]{1,0:T(8,128)(2,1)S(1)}, u32[]{:S(2)}, u32[]{:S(2)}) collective-permute-start(bf16[320,1024]{1,0:T(8,128)(2,1)S(1)} %fusion.refs_1_.refs_2_), channel_id=1, source_target_pairs={{0,4},{4,0},{8,12},{12,8},{16,20},{20,16},{24,28},{28,24},{1,5},{5... | collective-permute-start | bytes 1966088 | tf_op jit(solution)/shard_map/ppermute | solution.py:36
  19.9 19.7 %collective-permute-start.10 = (bf16[240,1024]{1,0:T(8,128)(2,1)S(1)}, bf16[240,1024]{1,0:T(8,128)(2,1)S(1)}, u32[]{:S(2)}, u32[]{:S(2)}) collective-permute-start(bf16[240,1024]{1,0:T(8,128)(2,1)S(1)} %slice.216), channel_id=1, source_target_pairs={{0,3},{1,2},{2,1},{3,0},{4,7},{5,6},{6,5},{7,4},{8,11},{9,10},{10,... | collective-permute-start | bytes 1474568 | tf_op jit(solution)/shard_map/ppermute | solution.py:36
  29.1 10.5 %collective-permute-start.6 = (f16[80,1792]{1,0:T(8,128)(2,1)S(1)}, f16[80,1792]{1,0:T(8,128)(2,1)S(1)}, u32[]{:S(2)}, u32[]{:S(2)}) collective-permute-start(f16[80,1792]{1,0:T(8,128)(2,1)S(1)} %get-tuple-element.195), channel_id=1, source_target_pairs={{0,8},{4,20},{8,0},{12,28},{16,24},{20,4},{24,16},{28,12},{1,9},{5... | collective-permute-start | bytes 860168 | tf_op jit(solution)/shard_map/ppermute | solution.py:42
  30.6 9.0 %collective-permute-start.7 = (f16[80,1792]{1,0:T(8,128)(2,1)S(1)}, f16[80,1792]{1,0:T(8,128)(2,1)S(1)}, u32[]{:S(2)}, u32[]{:S(2)}) collective-permute-start(f16[80,1792]{1,0:T(8,128)(2,1)S(1)} %get-tuple-element.194), channel_id=1, source_target_pairs={{0,8},{4,20},{8,0},{12,28},{16,24},{20,4},{24,16},{28,12},{1,9},{5... | collective-permute-start | bytes 860168 | tf_op jit(solution)/shard_map/ppermute | solution.py:42
  31.2 10.8 %collective-permute-start.8 = (f16[80,1792]{1,0:T(8,128)(2,1)S(1)}, f16[80,1792]{1,0:T(8,128)(2,1)S(1)}, u32[]{:S(2)}, u32[]{:S(2)}) collective-permute-start(f16[80,1792]{1,0:T(8,128)(2,1)S(1)} %get-tuple-element.193), channel_id=1, source_target_pairs={{0,8},{4,20},{8,0},{12,28},{16,24},{20,4},{24,16},{28,12},{1,9},{5... | collective-permute-start | bytes 860168 | tf_op jit(solution)/shard_map/ppermute | solution.py:42
  32.7 12.3 %collective-permute-start.9 = (f16[80,1792]{1,0:T(8,128)(2,1)S(1)}, f16[80,1792]{1,0:T(8,128)(2,1)S(1)}, u32[]{:S(2)}, u32[]{:S(2)}) collective-permute-start(f16[80,1792]{1,0:T(8,128)(2,1)S(1)} %get-tuple-element.192), channel_id=1, source_target_pairs={{0,8},{4,20},{8,0},{12,28},{16,24},{20,4},{24,16},{28,12},{1,9},{5... | collective-permute-start | bytes 860168 | tf_op jit(solution)/shard_map/ppermute | solution.py:42
  45.5 9.8 %collective-permute-start.11 = (f16[160,1792]{1,0:T(8,128)(2,1)S(1)}, f16[160,1792]{1,0:T(8,128)(2,1)S(1)}, u32[]{:S(2)}, u32[]{:S(2)}) collective-permute-start(f16[160,1792]{1,0:T(8,128)(2,1)S(1)} %pad_maximum_fusion.4), channel_id=1, source_target_pairs={{0,16},{4,12},{8,24},{12,4},{16,0},{20,28},{24,8},{28,20},{1,17},{... | collective-permute-start | bytes 1720328 | tf_op jit(solution)/shard_map/ppermute | solution.py:42
  55.6 9.5 %collective-permute-start.13 = (bf16[80,1792]{1,0:T(8,128)(2,1)S(1)}, bf16[80,1792]{1,0:T(8,128)(2,1)S(1)}, u32[]{:S(2)}, u32[]{:S(2)}) collective-permute-start(bf16[80,1792]{1,0:T(8,128)(2,1)S(1)} %multiply_convert_fusion.2), channel_id=1, source_target_pairs={{0,16},{4,12},{8,24},{12,4},{16,0},{20,28},{24,8},{28,20},{1,17},{... | collective-permute-start | bytes 860168 | tf_op jit(solution)/shard_map/ppermute | solution.py:42
  57.1 8.0 %collective-permute-start.14 = (bf16[80,1024]{1,0:T(8,128)(2,1)S(1)}, bf16[80,1024]{1,0:T(8,128)(2,1)S(1)}, u32[]{:S(2)}, u32[]{:S(2)}) collective-permute-start(bf16[80,1024]{1,0:T(8,128)(2,1)S(1)} %slice.217), channel_id=1, source_target_pairs={{0,3},{1,2},{2,1},{3,0},{4,7},{5,6},{6,5},{7,4},{8,11},{9,10},{10,... | collective-permute-start | bytes 491528 | tf_op jit(solution)/shard_map/ppermute | solution.py:36
  59.6 22.3 %collective-permute-start.19 = (f16[2,160,1792]{2,1,0:T(8,128)(2,1)}, f16[2,160,1792]{2,1,0:T(8,128)(2,1)}, u32[]{:S(2)}, u32[]{:S(2)}) collective-permute-start(f16[2,160,1792]{2,1,0:T(8,128)(2,1)} %convert_element_type.107), channel_id=1, source_target_pairs={{0,8},{4,20},{8,0},{12,28},{16,24},{20,4},{24,16},{28,12},{1,9},{5... | collective-permute-start | bytes 3440648 | tf_op jit(solution)/shard_map/ppermute | solution.py:42
  66.6 15.3 %collective-permute-start.15 = (bf16[160,1792]{1,0:T(8,128)(2,1)}, bf16[160,1792]{1,0:T(8,128)(2,1)}, u32[]{:S(2)}, u32[]{:S(2)}) collective-permute-start(bf16[160,1792]{1,0:T(8,128)(2,1)} %constant_dynamic-update-slice_fusion), channel_id=1, source_target_pairs={{0,8},{4,20},{8,0},{12,28},{16,24},{20,4},{24,16},{28,12},{1,9},{5... | collective-permute-start | bytes 1720328 | tf_op jit(solution)/shard_map/ppermute | solution.py:42
  67.4 17.1 %collective-permute-start.17 = (bf16[160,1792]{1,0:T(8,128)(2,1)}, bf16[160,1792]{1,0:T(8,128)(2,1)S(1)}, u32[]{:S(2)}, u32[]{:S(2)}) collective-permute-start(bf16[160,1792]{1,0:T(8,128)(2,1)} %constant_dynamic-update-slice_fusion), channel_id=1, source_target_pairs={{0,4},{4,0},{8,12},{12,8},{16,20},{20,16},{24,28},{28,24},{1,5},{5... | collective-permute-start | bytes 1720328 | tf_op jit(solution)/shard_map/ppermute | solution.py:36
  83.9 9.8 %collective-permute-start.20 = (f16[160,1792]{1,0:T(8,128)(2,1)S(1)}, f16[160,1792]{1,0:T(8,128)(2,1)S(1)}, u32[]{:S(2)}, u32[]{:S(2)}) collective-permute-start(f16[160,1792]{1,0:T(8,128)(2,1)S(1)} %pad_maximum_fusion.5), channel_id=1, source_target_pairs={{0,16},{4,12},{8,24},{12,4},{16,0},{20,28},{24,8},{28,20},{1,17},{... | collective-permute-start | bytes 1720328 | tf_op jit(solution)/shard_map/ppermute | solution.py:42
  92.7 10.9 %collective-permute-start.23 = (bf16[160,1024]{1,0:T(8,128)(2,1)}, bf16[160,1024]{1,0:T(8,128)(2,1)S(1)}, u32[]{:S(2)}, u32[]{:S(2)}) collective-permute-start(bf16[160,1024]{1,0:T(8,128)(2,1)} %fusion.6), channel_id=1, source_target_pairs={{0,1},{1,0},{2,3},{3,2},{4,5},{5,4},{6,7},{7,6},{8,9},{9,8},{10,11... | collective-permute-start | bytes 983048 | tf_op jit(solution)/shard_map/ppermute | solution.py:36
  93.9 6.7 %collective-permute-start.21 = (bf16[80,1792]{1,0:T(8,128)(2,1)S(1)}, bf16[80,1792]{1,0:T(8,128)(2,1)S(1)}, u32[]{:S(2)}, u32[]{:S(2)}) collective-permute-start(bf16[80,1792]{1,0:T(8,128)(2,1)S(1)} %multiply_convert_fusion.1), channel_id=1, source_target_pairs={{0,16},{4,12},{8,24},{12,4},{16,0},{20,28},{24,8},{28,20},{1,17},{... | collective-permute-start | bytes 860168 | tf_op jit(solution)/shard_map/ppermute | solution.py:42
  100.7 9.9 %collective-permute-start.22 = (bf16[160,1792]{1,0:T(8,128)(2,1)S(1)}, bf16[160,1792]{1,0:T(8,128)(2,1)}, u32[]{:S(2)}, u32[]{:S(2)}) collective-permute-start(bf16[160,1792]{1,0:T(8,128)(2,1)S(1)} %constant_dynamic-update-slice_fusion.2), channel_id=1, source_target_pairs={{0,8},{4,20},{8,0},{12,28},{16,24},{20,4},{24,16},{28,12},{1,9},{5... | collective-permute-start | bytes 1720328 | tf_op jit(solution)/shard_map/ppermute | solution.py:42
  103.5 10.6 %collective-permute-start.24 = (bf16[160,1792]{1,0:T(8,128)(2,1)S(1)}, bf16[160,1792]{1,0:T(8,128)(2,1)S(1)}, u32[]{:S(2)}, u32[]{:S(2)}) collective-permute-start(bf16[160,1792]{1,0:T(8,128)(2,1)S(1)} %constant_dynamic-update-slice_fusion.2), channel_id=1, source_target_pairs={{0,4},{4,0},{8,12},{12,8},{16,20},{20,16},{24,28},{28,24},{1,5},{5... | collective-permute-start | bytes 1720328 | tf_op jit(solution)/shard_map/ppermute | solution.py:36
  110.5 3.6 %collective-permute-start.25 = (bf16[160,1792]{1,0:T(8,128)(2,1)}, bf16[160,1792]{1,0:T(8,128)(2,1)S(1)}, u32[]{:S(2)}, u32[]{:S(2)}) collective-permute-start(bf16[160,1792]{1,0:T(8,128)(2,1)} %collective-permute-done.22), channel_id=1, source_target_pairs={{0,4},{4,0},{8,12},{12,8},{16,20},{20,16},{24,28},{28,24},{1,5},{5... | collective-permute-start | bytes 1720328 | tf_op jit(solution)/shard_map/ppermute | solution.py:36
  111.7 12.3 %collective-permute-start.27 = (bf16[160,1024]{1,0:T(8,128)(2,1)S(1)}, bf16[160,1024]{1,0:T(8,128)(2,1)S(1)}, u32[]{:S(2)}, u32[]{:S(2)}) collective-permute-start(bf16[160,1024]{1,0:T(8,128)(2,1)S(1)} %add_convert_fusion), channel_id=1, source_target_pairs={{0,3},{1,2},{2,1},{3,0},{4,7},{5,6},{6,5},{7,4},{8,11},{9,10},{10,... | collective-permute-start | bytes 983048 | tf_op jit(solution)/shard_map/ppermute | solution.py:36
  120.2 10.5 %collective-permute-start.26 = (bf16[160,1024]{1,0:T(8,128)(2,1)S(1)}, bf16[160,1024]{1,0:T(8,128)(2,1)S(1)}, u32[]{:S(2)}, u32[]{:S(2)}) collective-permute-start(bf16[160,1024]{1,0:T(8,128)(2,1)S(1)} %fusion.5), channel_id=1, source_target_pairs={{0,1},{1,0},{2,3},{3,2},{4,5},{5,4},{6,7},{7,6},{8,9},{9,8},{10,11... | collective-permute-start | bytes 983048 | tf_op jit(solution)/shard_map/ppermute | solution.py:36
  131.0 12.5 %collective-permute-start.29 = (bf16[160,1024]{1,0:T(8,128)(2,1)S(1)}, bf16[160,1024]{1,0:T(8,128)(2,1)S(1)}, u32[]{:S(2)}, u32[]{:S(2)}) collective-permute-start(bf16[160,1024]{1,0:T(8,128)(2,1)S(1)} %get-tuple-element.150.refs_6_), channel_id=1, source_target_pairs={{0,3},{1,2},{2,1},{3,0},{4,7},{5,6},{6,5},{7,4},{8,11},{9,10},{10,... | collective-permute-start | bytes 983048 | tf_op jit(solution)/shard_map/ppermute | solution.py:36
  133.6 16.0 %collective-permute-start.32 = (bf16[160,1024]{1,0:T(8,128)(2,1)S(1)}, bf16[160,1024]{1,0:T(8,128)(2,1)S(1)}, u32[]{:S(2)}, u32[]{:S(2)}) collective-permute-start(bf16[160,1024]{1,0:T(8,128)(2,1)S(1)} %get-tuple-element.150.refs_6_), channel_id=1, source_target_pairs={{0,1},{1,0},{2,3},{3,2},{4,5},{5,4},{6,7},{7,6},{8,9},{9,8},{10,11... | collective-permute-start | bytes 983048 | tf_op jit(solution)/shard_map/ppermute | solution.py:36
  135.0 3.7 %collective-permute-start.28 = (f32[8,128]{1,0:T(8,128)S(1)}, f32[8,128]{1,0:T(8,128)S(1)}, u32[]{:S(2)}, u32[]{:S(2)}) collective-permute-start(f32[8,128]{1,0:T(8,128)S(1)} %broadcast_in_dim.58), channel_id=1, source_target_pairs={{0,8},{4,12},{8,0},{12,4},{16,24},{20,28},{24,16},{28,20},{1,9},{5... | collective-permute-start | bytes 12296 | tf_op jit(solution)/shard_map/ppermute | solution.py:36
  143.5 14.6 %collective-permute-start.30 = (bf16[160,1024]{1,0:T(8,128)(2,1)S(1)}, bf16[160,1024]{1,0:T(8,128)(2,1)S(1)}, u32[]{:S(2)}, u32[]{:S(2)}) collective-permute-start(bf16[160,1024]{1,0:T(8,128)(2,1)S(1)} %collective-permute-done.29.refs_4_), channel_id=1, source_target_pairs={{0,1},{1,0},{2,3},{3,2},{4,5},{5,4},{6,7},{7,6},{8,9},{9,8},{10,11... | collective-permute-start | bytes 983048 | tf_op jit(solution)/shard_map/ppermute | solution.py:36
  153.6 16.0 %collective-permute-start.34 = (f32[8,128]{1,0:T(8,128)S(1)}, f32[8,128]{1,0:T(8,128)S(1)}, u32[]{:S(2)}, u32[]{:S(2)}) collective-permute-start(f32[8,128]{1,0:T(8,128)S(1)} %add.226), channel_id=1, source_target_pairs={{0,1},{1,0},{2,3},{3,2},{4,5},{5,4},{6,7},{7,6},{8,9},{9,8},{10,11... | collective-permute-start | bytes 12296 | tf_op jit(solution)/shard_map/ppermute | solution.py:36
  153.6 16.0 %collective-permute-start.35 = (f32[8,128]{1,0:T(8,128)S(1)}, f32[8,128]{1,0:T(8,128)S(1)}, u32[]{:S(2)}, u32[]{:S(2)}) collective-permute-start(f32[8,128]{1,0:T(8,128)S(1)} %add.226), channel_id=1, source_target_pairs={{0,2},{1,3},{2,0},{3,1},{4,6},{5,7},{6,4},{7,5},{8,10},{9,11},{10,... | collective-permute-start | bytes 12296 | tf_op jit(solution)/shard_map/ppermute | solution.py:36
  155.9 13.7 %collective-permute-start.36 = (f32[8,128]{1,0:T(8,128)S(1)}, f32[8,128]{1,0:T(8,128)S(1)}, u32[]{:S(2)}, u32[]{:S(2)}) collective-permute-start(f32[8,128]{1,0:T(8,128)S(1)} %add.226), channel_id=1, source_target_pairs={{0,3},{1,2},{2,1},{3,0},{4,7},{5,6},{6,5},{7,4},{8,11},{9,10},{10,... | collective-permute-start | bytes 12296 | tf_op jit(solution)/shard_map/ppermute | solution.py:36
  (27 other events, 124.8 us)
